TPU v7x, 32 devices: a whole 2x2x4 slice. The times are simulated.
32 devices in a mesh: dp: 8 (over z, y), tensor: 4 (over x, core).
Axes of the slice: x: 2, y: 2, z: 4, core: 2. Of those that a mesh axis runs over, the one named last changes fastest.
Arguments:
- layer_input: bfloat16 [10240, 768], P(('dp', 'tensor')), may hold values from -6 to 6
- cotangent: bfloat16 [10240, 768], P(('dp', 'tensor')), may hold values from -6 to 6
- segments: int32 [10240], replicated, may hold values from 0 to 25, as said below
- parents: int32 [26], replicated, may hold values from 0 to 17, as said below
- norm1_gain: bfloat16 [768], P('dp'), may hold values from 0.099609375 to 1.8984375
- w_query: bfloat16 [768, 768], P('dp', 'tensor'), may hold values from -0.21875 to 0.21875
- w_key: bfloat16 [768, 768], P('dp', 'tensor'), may hold values from -0.21875 to 0.21875
- w_value: bfloat16 [768, 768], P('dp', 'tensor'), may hold values from -0.21875 to 0.21875
- w_out: bfloat16 [768, 768], P('tensor', 'dp'), may hold values from -1.75 to 1.75
- norm2_gain: bfloat16 [768], P('dp'), may hold values from 0.099609375 to 1.8984375
- w_up: bfloat16 [768, 3072], P('dp', 'tensor'), may hold values from -0.21875 to 0.21875
- w_down: bfloat16 [3072, 768], P('tensor', 'dp'), may hold values from -0.109375 to 0.109375
Outputs:
- layer_output: bfloat16 [10240, 768], P(('dp', 'tensor'))
- input_grad: bfloat16 [10240, 768], P(('dp', 'tensor'))
- grad_norm1_gain: float32 [768], P('dp')
- grad_query: float32 [768, 768], P('dp', 'tensor')
- grad_key: float32 [768, 768], P('dp', 'tensor')
- grad_value: float32 [768, 768], P('dp', 'tensor')
- grad_out: float32 [768, 768], P('tensor', 'dp')
- grad_norm2_gain: float32 [768], P('dp')
- grad_up: float32 [768, 3072], P('dp', 'tensor')
- grad_down: float32 [3072, 768], P('tensor', 'dp')
Inputs may be any that keep to these rules, and one draw needn't show every extreme that they name: Tree t holds bytes 5120 t to 5120 (t + 1) - 1 of the stream (the last tree may end at 10240). Its first 2048 bytes are segment 13 t, the trunk; the rest are twelve runs of 256 bytes with the segments 13 t + 1 to 13 t + 12 in some order, every run after the run of its parent segment. parents[s] is the parent segment of s: the trunk 13 t is its own parent, the branches 13 t + 1 to 13 t + 4 have the trunk, and the leaves 13 t + 5 to 13 t + 12 have one of the four branches each, two leaves a branch.
All inputs are finite; a program needn't handle non-finite values.
Results may differ from a plain program's by a relative error of at most 0.017.
Values may be sent and summed in bfloat16 or wider, within the bound.
A program may use at most 256 MiB of HBM per device.

v0:
```python
import math
import jax
import jax.numpy as jnp
from jax import lax
from jax.sharding import PartitionSpec as P

HD = 64
WINDOW = 1536
epsilon = 1e-06
masked_score = -1e30


def from_behind(block, axis, distance):
    devices = range(lax.axis_size(axis))
    route = [(i - distance, i) for i in devices if i - distance in devices]
    return lax.ppermute(block, axis, route)


def split_up(x, dim, peers):
    dims = x.shape
    tiles = x.reshape(*dims[:dim], peers, dims[dim] // peers, *dims[dim + 1 :])
    return jnp.moveaxis(tiles, dim, 0)


def sum_at_owner(x, axis, dim):
    tiles = split_up(x, dim, lax.axis_size(axis))
    arrived = lax.all_to_all(tiles, axis, split_axis=0, concat_axis=0, tiled=True)
    return arrived.astype(jnp.float32).sum(axis=0)


def side_by_side(arrays, axis, dim, along):
    widths = [math.prod(a.shape[along:]) for a in arrays]
    both = jnp.concatenate(
        [a.reshape(*a.shape[:along], w) for a, w in zip(arrays, widths)], axis=along
    )
    whole = sum_at_owner(both, axis, dim)
    tiles = jnp.split(whole, [sum(widths[:k]) for k in range(1, len(widths))], axis=along)
    return tuple((b.reshape(*whole.shape[:along], *a.shape[along:]) for a, b in zip(arrays, tiles)))


def gelu_exact(values):
    return jax.nn.gelu(values, approximate=False)


def row_scale(values):
    return lax.rsqrt(jnp.mean(values * values, axis=-1, keepdims=True) + epsilon)


def norm_backward(incoming, normal_hat, row_factor, gain):
    scaled = incoming * gain
    inner = jnp.mean(scaled * normal_hat, axis=-1, keepdims=True)
    return (row_factor * (scaled - normal_hat * inner), jnp.sum(incoming * normal_hat, axis=0))


def parent_of(seg_ids, parents):
    seg_table = jnp.arange(parents.shape[0], dtype=jnp.int32)
    hits = seg_ids[:, None] == seg_table[None, :]
    return jnp.sum(jnp.where(hits, parents[None, :], 0), axis=1)


def shards(
    layer_input,
    cotangent,
    segments,
    parents,
    norm1_gain,
    w_query,
    w_key,
    w_value,
    w_out,
    norm2_gain,
    w_up,
    w_down,
):
    gain_one, full_query, full_key, full_value, full_out, gain_two, full_up, full_down = (
        lax.all_gather(norm1_gain, "dp", axis=0, tiled=True),
        lax.all_gather(w_query, "dp", axis=0, tiled=True),
        lax.all_gather(w_key, "dp", axis=0, tiled=True),
        lax.all_gather(w_value, "dp", axis=0, tiled=True),
        lax.all_gather(w_out, "dp", axis=1, tiled=True),
        lax.all_gather(norm2_gain, "dp", axis=0, tiled=True),
        lax.all_gather(w_up, "dp", axis=0, tiled=True),
        lax.all_gather(w_down, "dp", axis=1, tiled=True),
    )
    gain_one = gain_one.astype(jnp.float32)
    gain_two = gain_two.astype(jnp.float32)
    row_count = layer_input.shape[0]
    token_count = row_count * lax.axis_size("tensor")
    position = lax.axis_index("dp") * token_count
    head_width = full_query.shape[1]
    head_count = head_width // HD
    scaling = HD ** (-0.5)
    block_rows = min(640, token_count)
    block_count = token_count // block_rows
    span = WINDOW + block_rows
    hop_count = (WINDOW + token_count - 1) // token_count
    inputs = layer_input.astype(jnp.float32)
    factor_one = row_scale(inputs)
    hat_one = inputs * factor_one
    normed = (hat_one * gain_one).astype(jnp.bfloat16)
    normed_all = lax.all_gather(normed, "tensor", axis=0, tiled=True)
    queries = jnp.dot(normed_all, full_query, preferred_element_type=jnp.float32).astype(
        jnp.bfloat16
    )
    keys_own = jnp.dot(normed_all, full_key, preferred_element_type=jnp.float32).astype(
        jnp.bfloat16
    )
    values_own = jnp.dot(normed_all, full_value, preferred_element_type=jnp.float32).astype(
        jnp.bfloat16
    )
    pair_own = jnp.concatenate([keys_own, values_own], axis=1)
    halo_parts = []
    for distance in range(1, hop_count + 1):
        length = min(token_count, WINDOW - (distance - 1) * token_count)
        piece = pair_own[token_count - length :]
        moved = from_behind(piece, "dp", distance)
        halo_parts.append(moved)
    pair_all = jnp.concatenate(halo_parts[::-1] + [pair_own], axis=0)
    seg_padded = jnp.concatenate([jnp.full((WINDOW,), -1, jnp.int32), segments])
    seg_keys = lax.dynamic_slice_in_dim(seg_padded, position, WINDOW + token_count, 0)
    seg_query = seg_keys[WINDOW:]
    parent_one = parent_of(seg_query, parents)
    parent_two = parent_of(parent_one, parents)
    query_spots = jnp.arange(block_rows, dtype=jnp.int32)
    key_spots = jnp.arange(span, dtype=jnp.int32)

    def scores_of(offset):
        query_block = lax.dynamic_slice_in_dim(queries, offset, block_rows, 0).reshape(
            block_rows, head_count, HD
        )
        pair_block = lax.dynamic_slice_in_dim(pair_all, offset, span, 0)
        key_block = pair_block[:, :head_width].reshape(span, head_count, HD)
        value_block = pair_block[:, head_width:].reshape(span, head_count, HD)
        own_seg = lax.dynamic_slice_in_dim(seg_query, offset, block_rows, 0)
        up_one = lax.dynamic_slice_in_dim(parent_one, offset, block_rows, 0)
        up_two = lax.dynamic_slice_in_dim(parent_two, offset, block_rows, 0)
        near_seg = lax.dynamic_slice_in_dim(seg_keys, offset, span, 0)
        gap = WINDOW + query_spots[:, None] - key_spots[None, :]
        same_path = (
            (near_seg[None, :] == own_seg[:, None])
            | (near_seg[None, :] == up_one[:, None])
            | (near_seg[None, :] == up_two[:, None])
        )
        allowed = (gap >= 0) & (gap < WINDOW) & same_path
        raw = (
            jnp.einsum("qhd,khd->hqk", query_block, key_block, preferred_element_type=jnp.float32)
            * scaling
        )
        return (jnp.where(allowed[None], raw, masked_score), query_block, key_block, value_block)

    def forward_block(block_index):
        scores, query_block, key_block, value_block = scores_of(block_index * block_rows)
        row_max = jnp.max(scores, axis=-1, keepdims=True)
        exponent = jnp.exp(scores - row_max)
        denominator = jnp.sum(exponent, axis=-1, keepdims=True)
        weights = (exponent / denominator).astype(jnp.bfloat16)
        mixed = jnp.einsum("hqk,khd->qhd", weights, value_block, preferred_element_type=jnp.float32)
        return (
            mixed.reshape(block_rows, head_width).astype(jnp.bfloat16),
            (row_max + jnp.log(denominator))[..., 0],
        )

    context_blocks, logsum_blocks = lax.map(forward_block, jnp.arange(block_count, dtype=jnp.int32))
    context = context_blocks.reshape(token_count, head_width)
    middle = inputs + lax.psum_scatter(
        jnp.dot(context, full_out, preferred_element_type=jnp.float32).astype(jnp.bfloat16),
        "tensor",
        scatter_dimension=0,
        tiled=True,
    ).astype(jnp.float32)
    factor_two = row_scale(middle)
    hat_two = middle * factor_two
    normed_two = (hat_two * gain_two).astype(jnp.bfloat16)
    normed_two_all = lax.all_gather(normed_two, "tensor", axis=0, tiled=True)
    upper = jnp.dot(normed_two_all, full_up, preferred_element_type=jnp.float32)
    active = gelu_exact(upper).astype(jnp.bfloat16)
    result = middle + lax.psum_scatter(
        jnp.dot(active, full_down, preferred_element_type=jnp.float32).astype(jnp.bfloat16),
        "tensor",
        scatter_dimension=0,
        tiled=True,
    ).astype(jnp.float32)
    incoming = cotangent.astype(jnp.float32)
    incoming_all = lax.all_gather(cotangent, "tensor", axis=0, tiled=True)
    grad_down = jnp.einsum("tf,td->fd", active, incoming_all, preferred_element_type=jnp.float32)
    grad_active = jnp.einsum(
        "td,fd->tf", incoming_all, full_down, preferred_element_type=jnp.float32
    )
    unused_value, gelu_pull = jax.vjp(gelu_exact, upper)
    grad_upper = gelu_pull(grad_active)[0].astype(jnp.bfloat16)
    grad_up = jnp.einsum(
        "tc,tf->cf", normed_two_all, grad_upper, preferred_element_type=jnp.float32
    )
    grad_normed_two = lax.psum_scatter(
        jnp.einsum("tf,cf->tc", grad_upper, full_up, preferred_element_type=jnp.float32).astype(
            jnp.bfloat16
        ),
        "tensor",
        scatter_dimension=0,
        tiled=True,
    ).astype(jnp.float32)
    through_two, gain_two_part = norm_backward(grad_normed_two, hat_two, factor_two, gain_two)
    grad_middle = incoming + through_two
    grad_middle_all = lax.all_gather(grad_middle.astype(jnp.bfloat16), "tensor", axis=0, tiled=True)
    grad_out = jnp.einsum("tc,td->cd", context, grad_middle_all, preferred_element_type=jnp.float32)
    grad_context = jnp.einsum(
        "td,cd->tc", grad_middle_all, full_out, preferred_element_type=jnp.float32
    ).astype(jnp.bfloat16)

    def backward_block(block_index, carry):
        grad_queries, grad_pairs = carry
        offset = block_index * block_rows
        scores, query_block, key_block, value_block = scores_of(offset)
        logsum = lax.dynamic_index_in_dim(logsum_blocks, block_index, 0, keepdims=False)
        probs = jnp.exp(scores - logsum[..., None])
        grad_rows = lax.dynamic_slice_in_dim(grad_context, offset, block_rows, 0).reshape(
            block_rows, head_count, HD
        )
        grad_probs = jnp.einsum(
            "qhd,khd->hqk", grad_rows, value_block, preferred_element_type=jnp.float32
        )
        inner = jnp.sum(probs * grad_probs, axis=-1, keepdims=True)
        grad_scores = (probs * (grad_probs - inner)).astype(jnp.bfloat16)
        grad_query_block = (
            jnp.einsum("hqk,khd->qhd", grad_scores, key_block, preferred_element_type=jnp.float32)
            * scaling
        )
        grad_key_block = (
            jnp.einsum("hqk,qhd->khd", grad_scores, query_block, preferred_element_type=jnp.float32)
            * scaling
        )
        grad_value_block = jnp.einsum(
            "hqk,qhd->khd",
            probs.astype(jnp.bfloat16),
            grad_rows,
            preferred_element_type=jnp.float32,
        )
        grad_queries = lax.dynamic_update_slice_in_dim(
            grad_queries, grad_query_block.reshape(block_rows, head_width), offset, 0
        )
        update = jnp.concatenate(
            [grad_key_block.reshape(span, head_width), grad_value_block.reshape(span, head_width)],
            axis=1,
        )
        current = lax.dynamic_slice_in_dim(grad_pairs, offset, span, 0)
        grad_pairs = lax.dynamic_update_slice_in_dim(grad_pairs, current + update, offset, 0)
        return (grad_queries, grad_pairs)

    start_carry = (
        jnp.zeros((token_count, head_width), jnp.float32),
        jnp.zeros((WINDOW + token_count, 2 * head_width), jnp.float32),
    )
    grad_queries, grad_pairs = lax.fori_loop(0, block_count, backward_block, start_carry)
    grad_own = grad_pairs[WINDOW:]
    for distance in range(1, hop_count + 1):
        length = min(token_count, WINDOW - (distance - 1) * token_count)
        first_row = WINDOW - (distance - 1) * token_count - length
        piece = grad_pairs[first_row : first_row + length]
        returned = from_behind(piece.astype(jnp.bfloat16), "dp", -distance).astype(piece.dtype)
        grad_own = grad_own + jnp.pad(returned, ((token_count - length, 0), (0, 0)))
    grad_keys = grad_own[:, :head_width].astype(jnp.bfloat16)
    grad_values = grad_own[:, head_width:].astype(jnp.bfloat16)
    grad_queries_low = grad_queries.astype(jnp.bfloat16)
    grad_query = jnp.einsum(
        "tc,tq->cq", normed_all, grad_queries_low, preferred_element_type=jnp.float32
    )
    grad_key = jnp.einsum("tc,tq->cq", normed_all, grad_keys, preferred_element_type=jnp.float32)
    grad_value = jnp.einsum(
        "tc,tq->cq", normed_all, grad_values, preferred_element_type=jnp.float32
    )
    part_query = jnp.einsum(
        "tq,cq->tc", grad_queries_low, full_query, preferred_element_type=jnp.float32
    )
    part_key = jnp.einsum("tq,cq->tc", grad_keys, full_key, preferred_element_type=jnp.float32)
    part_value = jnp.einsum(
        "tq,cq->tc", grad_values, full_value, preferred_element_type=jnp.float32
    )
    grad_normed = lax.psum_scatter(
        (part_query + part_key + part_value).astype(jnp.bfloat16),
        "tensor",
        scatter_dimension=0,
        tiled=True,
    ).astype(jnp.float32)
    through_one, gain_one_part = norm_backward(grad_normed, hat_one, factor_one, gain_one)
    grad_inputs = grad_middle + through_one
    gain_one_sum, gain_two_sum = lax.psum((gain_one_part, gain_two_part), "tensor")
    summed = (
        *side_by_side(
            (
                gain_one_sum.astype(jnp.bfloat16),
                grad_query.astype(jnp.bfloat16),
                grad_key.astype(jnp.bfloat16),
                grad_value.astype(jnp.bfloat16),
            ),
            "dp",
            0,
            1,
        ),
        sum_at_owner(grad_out.astype(jnp.bfloat16), "dp", 1),
        *side_by_side(
            (gain_two_sum.astype(jnp.bfloat16), grad_up.astype(jnp.bfloat16)), "dp", 0, 1
        ),
        sum_at_owner(grad_down.astype(jnp.bfloat16), "dp", 1),
    )
    return (
        result.astype(jnp.bfloat16),
        grad_inputs.astype(jnp.bfloat16),
        summed[0],
        summed[1],
        summed[2],
        summed[3],
        summed[4],
        summed[5],
        summed[6],
        summed[7],
    )


def solution(mesh):
    return jax.shard_map(
        shards,
        mesh=mesh,
        in_specs=(
            P(("dp", "tensor"), None),
            P(("dp", "tensor"), None),
            P(),
            P(),
            P("dp"),
            P("dp", "tensor"),
            P("dp", "tensor"),
            P("dp", "tensor"),
            P("tensor", "dp"),
            P("dp"),
            P("dp", "tensor"),
            P("tensor", "dp"),
        ),
        out_specs=(
            P(("dp", "tensor"), None),
            P(("dp", "tensor"), None),
            P("dp"),
            P("dp", "tensor"),
            P("dp", "tensor"),
            P("dp", "tensor"),
            P("tensor", "dp"),
            P("dp"),
            P("dp", "tensor"),
            P("tensor", "dp"),
        ),
        check_vma=False,
    )
```

profile of v0, /device:TPU:0, one launch (start us, length us, event | category | flops | bytes accessed | tf_op | source)
XLA Modules:
  0.0 772.6 jit_solution(16327131825716059331)
XLA Ops:
  12.9 23.7 %all-reduce.5 = (bf16[768]{0:T(1024)(128)(2,1)S(1)}, bf16[768]{0:T(1024)(128)(2,1)}) all-reduce(bf16[768]{0:T(1024)(128)(2,1)S(1)} %dynamic-update-slice, bf16[768]{0:T(1024)(128)(2,1)S(1)} %dynamic-update-slice.1), channel_id=1, replica_groups=mesh['dp'=8,'tensor'=4] {'dp'}, use_global_device_ids=true, to_apply=%add.2 | all-reduce | flops 1536 | bytes 6144
  41.0 31.2 %all_gather.38 = bf16[768,192]{1,0:T(8,128)(2,1)S(1)} all-gather(bf16[96,192]{1,0:T(8,128)(2,1)} %param.22), channel_id=1, replica_groups=mesh['dp'=8,'tensor'=4] {'dp'}, dimensions={0}, use_global_device_ids=true | all-gather | bytes 331776 | tf_op jit(solution)/shard_map/all_gather | solution.py:78
  72.2 31.2 %all_gather.39 = bf16[768,192]{1,0:T(8,128)(2,1)S(1)} all-gather(bf16[96,192]{1,0:T(8,128)(2,1)} %param.23), channel_id=1, replica_groups=mesh['dp'=8,'tensor'=4] {'dp'}, dimensions={0}, use_global_device_ids=true | all-gather | bytes 331776 | tf_op jit(solution)/shard_map/all_gather | solution.py:79
  110.2 46.0 %all_gather.41 = bf16[192,768]{0,1:T(8,128)(2,1)} all-gather(bf16[192,96]{0,1:T(8,128)(2,1)S(1)} %copy.48), channel_id=1, replica_groups=mesh['dp'=8,'tensor'=4] {'dp'}, dimensions={1}, use_global_device_ids=true | all-gather | bytes 331776 | tf_op jit(solution)/shard_map/all_gather | solution.py:80
  156.2 31.0 %all_gather.40 = bf16[768,192]{1,0:T(8,128)(2,1)S(1)} all-gather(bf16[96,192]{1,0:T(8,128)(2,1)S(1)} %copy-done.35), channel_id=1, replica_groups=mesh['dp'=8,'tensor'=4] {'dp'}, dimensions={0}, use_global_device_ids=true | all-gather | bytes 331776 | tf_op jit(solution)/shard_map/all_gather | solution.py:77
  193.2 72.5 %while.29 = (s32[]{:T(128)}, bf16[2,640,192]{1,2,0:T(8,128)(2,1)}, f32[2,3,640]{2,1,0:T(4,128)S(1)}, s32[2]{0:T(128)S(1)}, bf16[2816,384]{0,1:T(8,128)(2,1)}, /*...) while((s32[]{:T(128)}, bf16[2,640,192]{1,2,0:T(8,128)(2,1)}, ...), condition=%wide.region_6.7_spmd.clone, body=%wide.region_3.6_spmd.clone.sunk | while | flops 1133730560 | bytes 66249560 | solution.py:163
  209.3 10.5 %fusion.137 = f32[3,640]{1,0:T(4,128)S(1)} fusion(f32[3,640,2176]{2,1,0:T(8,128)} %get-tuple-element.566, f32[3,640]{1,0:T(4,128)S(1)} %get-tuple-element.567, pred[640,2176]{1,0:T(8,128)(4,1)S(1)} %fusion.135), kind=kLoop, calls=%fused_computation.8.clone.1 | loop fusion | flops 16709760 | bytes 18119680 | tf_op jit(solution)/shard_map/while/body/eval_jaxpr/reduce_sum | solution.py:155
  245.5 10.5 %fusion.137 = f32[3,640]{1,0:T(4,128)S(1)} fusion(f32[3,640,2176]{2,1,0:T(8,128)} %get-tuple-element.566, f32[3,640]{1,0:T(4,128)S(1)} %get-tuple-element.567, pred[640,2176]{1,0:T(8,128)(4,1)S(1)} %fusion.135), kind=kLoop, calls=%fused_computation.8.clone.1 | loop fusion | flops 16709760 | bytes 18119680 | tf_op jit(solution)/shard_map/while/body/eval_jaxpr/reduce_sum | solution.py:155
  271.0 32.7 %reduce-scatter.5.cloned.1.call-done = bf16[320,768]{1,0:T(8,128)(2,1)} async-done(((bf16[1280,768]{1,0:T(8,128)(2,1)}), bf16[320,768]{1,0:T(8,128)(2,1)}) %reduce-scatter.5.cloned.1.call-update) | async-done | bytes 491536 | tf_op jit(solution)/shard_map/reduce_scatter | solution.py:165
  317.4 22.3 %all-gather.9.cloned.1.call-done = bf16[1280,768]{1,0:T(8,128)(2,1)} async-done(((bf16[320,768]{1,0:T(8,128)(2,1)}), bf16[1280,768]{1,0:T(8,128)(2,1)}) %all-gather.9.cloned.1.call-update) | async-done | bytes 1966096 | tf_op jit(solution)/shard_map/all_gather | solution.py:174
  345.1 38.4 %all-gather.13.cloned.1.call-done = bf16[768,768]{0,1:T(8,128)(2,1)} async-done(((bf16[768,96]{0,1:T(8,128)(2,1)}), bf16[768,768]{0,1:T(8,128)(2,1)}) %all-gather.13.cloned.1.call-update) | async-done | bytes 1179664 | tf_op jit(solution)/shard_map/all_gather | solution.py:83
  383.5 21.9 %all-gather.15.cloned.1.call-done = bf16[1280,768]{1,0:T(8,128)(2,1)} async-done(((bf16[320,768]{1,0:T(8,128)(2,1)}), bf16[1280,768]{1,0:T(8,128)(2,1)}) %all-gather.15.cloned.1.call-update) | async-done | bytes 1966096 | tf_op jit(solution)/shard_map/all_gather | solution.py:184
  405.4 13.1 %add_convert_fusion = (bf16[1280,768]{1,0:T(8,128)(2,1)S(1)}, f32[1280,768]{1,0:T(8,128)}) fusion(f32[1280,768]{1,0:T(8,128)} %fusion.64, bf16[1280,768]{1,0:T(8,128)(2,1)} %all-gather.15.cloned.1.call-done, bf16[768,768]{0,1:T(8,128)(2,1)} %all-gather.13.cloned.1.call-done), kind=kOutput, calls=%fused_computation.47 | convolution fusion | flops 1580728320 | bytes 12976128 | tf_op jit(solution)/shard_map/td,fd->tf/dot_general | solution.py:186
  424.3 30.7 %reduce-scatter.9.cloned.1.call-done = bf16[320,768]{1,0:T(8,128)(2,1)} async-done(((bf16[1280,768]{1,0:T(8,128)(2,1)}), bf16[320,768]{1,0:T(8,128)(2,1)}) %reduce-scatter.9.cloned.1.call-update) | async-done | bytes 491536 | tf_op jit(solution)/shard_map/reduce_scatter | solution.py:194
  459.9 21.4 %all-gather.17.cloned.1.call-done = bf16[1280,768]{1,0:T(8,128)(2,1)} async-done(((bf16[320,768]{1,0:T(8,128)(2,1)}), bf16[1280,768]{1,0:T(8,128)(2,1)}) %all-gather.17.cloned.1.call-update) | async-done | bytes 1966096 | tf_op jit(solution)/shard_map/all_gather | solution.py:204
  487.6 112.6 %while.30 = (s32[]{:T(128)}, bf16[1280,192]{0,1:T(8,128)(2,1)}, f32[2816,384]{0,1:T(8,128)}, bf16[2816,384]{0,1:T(8,128)(2,1)}, s32[2816]{0:T(1024)S(1)}, /*inde...) while((s32[]{:T(128)}, bf16[1280,192]{0,1:T(8,128)(2,1)}, ...), condition=%wide.region_14.15_spmd.clone, body=%wide.region_12.14_spmd.clone.sunk | while | flops 2727729920 | bytes 220916592 | solution.py:253
  503.3 15.1 %multiply_reduce_fusion.3 = (f32[3,640]{1,0:T(4,128)S(1)}, f32[3,640,2176]{2,1,0:T(8,128)}) fusion(f32[3,640,2176]{2,1,0:T(8,128)} %fusion.150, f32[3,640]{1,0:T(4,128)S(1)} %dynamic-slice_bitcast_fusion.2, bf16[640,3,64]{0,2,1:T(8,128)(2,1)S(1)} %bitcast.138, bf16[2176,3,64]{0,2,1:T(8,128)(2,1)S(1)} %bitcast.135, pred[640,2176]{1,0:T(8,128)(4,1)S(1)} %fusion.151), kind=kOutput, calls=%fused_computation.24.clone.1 | convolution fusion | flops 555661440 | bytes 35912704 | tf_op jit(solution)/shard_map/while/body/eval_jaxpr/qhd,khd->hqk/dot_general | solution.py:146
  518.5 11.4 %multiply_convert_fusion.4 = bf16[3,640,2176]{2,1,0:T(8,128)(2,1)S(1)} fusion(f32[3,640,2176]{2,1,0:T(8,128)} %get-tuple-element.583, f32[3,640,2176]{2,1,0:T(8,128)} %fusion.150, f32[3,640]{1,0:T(4,128)S(1)} %get-tuple-element.584), kind=kLoop, calls=%fused_computation.23.clone.1 | loop fusion | flops 12533760 | bytes 41786880 | tf_op jit(solution)/shard_map/while/body/eval_jaxpr/convert_element_type | solution.py:223
  559.6 15.1 %multiply_reduce_fusion.3 = (f32[3,640]{1,0:T(4,128)S(1)}, f32[3,640,2176]{2,1,0:T(8,128)}) fusion(f32[3,640,2176]{2,1,0:T(8,128)} %fusion.150, f32[3,640]{1,0:T(4,128)S(1)} %dynamic-slice_bitcast_fusion.2, bf16[640,3,64]{0,2,1:T(8,128)(2,1)S(1)} %bitcast.138, bf16[2176,3,64]{0,2,1:T(8,128)(2,1)S(1)} %bitcast.135, pred[640,2176]{1,0:T(8,128)(4,1)S(1)} %fusion.151), kind=kOutput, calls=%fused_computation.24.clone.1 | convolution fusion | flops 555661440 | bytes 35912704 | tf_op jit(solution)/shard_map/while/body/eval_jaxpr/qhd,khd->hqk/dot_general | solution.py:146
  574.7 11.4 %multiply_convert_fusion.4 = bf16[3,640,2176]{2,1,0:T(8,128)(2,1)S(1)} fusion(f32[3,640,2176]{2,1,0:T(8,128)} %get-tuple-element.583, f32[3,640,2176]{2,1,0:T(8,128)} %fusion.150, f32[3,640]{1,0:T(4,128)S(1)} %get-tuple-element.584), kind=kLoop, calls=%fused_computation.23.clone.1 | loop fusion | flops 12533760 | bytes 41786880 | tf_op jit(solution)/shard_map/while/body/eval_jaxpr/convert_element_type | solution.py:223
  606.3 27.3 %collective-permute-done.3 = bf16[256,384]{0,1:T(8,128)(2,1)S(1)} collective-permute-done((bf16[256,384]{0,1:T(8,128)(2,1)S(1)}, bf16[256,384]{0,1:T(8,128)(2,1)S(1)}, u32[]{:S(2)}, u32[]{:S(2)}) %collective-permute-start.3) | collective-permute-done | bytes 196640 | tf_op jit(solution)/shard_map/ppermute | solution.py:16
  667.0 11.4 %all-to-all-done.3 = bf16[8,768,96]{1,2,0:T(8,128)(2,1)} async-done(((bf16[8,768,96]{1,2,0:T(8,128)(2,1)}), bf16[8,768,96]{1,2,0:T(8,128)(2,1)}, u32[]{:S(2)}, u32[]{:S(2)}) %all-to-all-start.3) | async-done | bytes 1179680 | tf_op jit(solution)/shard_map/all_to_all | solution.py:27
  710.6 15.5 %all-to-all-done = bf16[8,96,577]{2,1,0:T(8,128)(2,1)S(1)} async-done(((bf16[8,96,577]{2,1,0:T(8,128)(2,1)}), bf16[8,96,577]{2,1,0:T(8,128)(2,1)S(1)}, u32[]{:S(2)}, u32[]{:S(2)}) %all-to-all-start) | async-done | bytes 886304 | tf_op jit(solution)/shard_map/all_to_all | solution.py:27
  739.1 24.3 %all-to-all-done.2 = bf16[8,96,769]{2,1,0:T(8,128)(2,1)S(1)} async-done(((bf16[8,96,769]{2,1,0:T(8,128)(2,1)}), bf16[8,96,769]{2,1,0:T(8,128)(2,1)S(1)}, u32[]{:S(2)}, u32[]{:S(2)}) %all-to-all-start.2) | async-done | bytes 1181216 | tf_op jit(solution)/shard_map/all_to_all | solution.py:27
  (266 shorter events, 257.7 us)
Async XLA Ops:
  8.0 95.4 %all-gather.7.cloned.1.call-start = ((), (), s32[]{:S(2)}) async-start(), calls=%async_computation.8 | async-start | bytes 2457600 | tf_op jit(solution)/shard_map/all_gather | solution.py:101
  39.2 264.5 %reduce-scatter.5.cloned.1.call-start = ((), (), s32[]{:S(2)}) async-start(), calls=%async_computation.9 | async-start | bytes 2457600 | tf_op jit(solution)/shard_map/reduce_scatter | solution.py:165
  103.4 52.9 %copy-start.21 = (bf16[768,192]{1,0:T(8,128)(2,1)}, bf16[768,192]{1,0:T(8,128)(2,1)S(1)}, u32[]{:S(2)}) copy-start(bf16[768,192]{1,0:T(8,128)(2,1)S(1)} %all_gather.39) | copy-start | bytes 884740
  103.4 52.9 %copy-start.35 = (bf16[96,192]{1,0:T(8,128)(2,1)S(1)}, bf16[96,192]{1,0:T(8,128)(2,1)}, u32[]{:S(2)}) copy-start(bf16[96,192]{1,0:T(8,128)(2,1)} %param.21) | copy-start | bytes 110596
  105.9 82.6 %copy-start.3 = (bf16[1280,768]{1,0:T(8,128)(2,1)S(1)}, bf16[1280,768]{1,0:T(8,128)(2,1)}, u32[]{:S(2)}) copy-start(bf16[1280,768]{1,0:T(8,128)(2,1)} %all-gather.7.cloned.1.call-done) | copy-start | bytes 5898244
  108.5 83.2 %collective-permute-start.1 = (bf16[1280,384]{0,1:T(8,128)(2,1)S(1)}, bf16[1280,384]{0,1:T(8,128)(2,1)S(1)}, u32[]{:S(2)}, u32[]{:S(2)}) collective-permute-start(bf16[1280,384]{0,1:T(8,128)(2,1)S(1)} %pad_maximum_fusion.1), channel_id=1, source_target_pairs={{0,4},{4,8},{8,12},{12,16},{16,20},{20,24},{24,28},{1,5},{5,9},{9,... | collective-permute-start | bytes 2949128 | tf_op jit(solution)/shard_map/ppermute | solution.py:16
  187.2 4.5 collective-permute-start
  270.1 47.3 %all-gather.11.cloned.1.call-start = ((), (), s32[]{:S(2)}) async-start(), calls=%async_computation.11 | async-start | bytes 1327104 | tf_op jit(solution)/shard_map/all_gather | solution.py:82
  270.7 69.0 %all-gather.9.cloned.1.call-start = ((), (), s32[]{:S(2)}) async-start(), calls=%async_computation.10 | async-start | bytes 2457600 | tf_op jit(solution)/shard_map/all_gather | solution.py:174
  271.0 186.2 %copy-start.29 = (f32[768]{0:T(1024)}, f32[768]{0:T(1024)S(1)}, u32[]{:S(2)}) copy-start(f32[768]{0:T(1024)S(1)} %convert_element_type.159) | copy-start | bytes 9220
  305.0 152.2 %copy-start.33 = (f32[320]{0:T(512)}, f32[320]{0:T(512)S(1)}, u32[]{:S(2)}) copy-start(f32[320]{0:T(512)S(1)} %add_rsqrt_fusion) | copy-start | bytes 3844
  307.1 76.4 %all-gather.13.cloned.1.call-start = ((), (), s32[]{:S(2)}) async-start(), calls=%async_computation.12 | async-start | bytes 1327104 | tf_op jit(solution)/shard_map/all_gather | solution.py:83
  307.6 97.7 %all-gather.15.cloned.1.call-start = ((), (), s32[]{:S(2)}) async-start(), calls=%async_computation.14 | async-start | bytes 2457600 | tf_op jit(solution)/shard_map/all_gather | solution.py:184
  308.4 146.7 %reduce-scatter.9.cloned.1.call-start = ((), (), s32[]{:S(2)}) async-start(), calls=%async_computation.15 | async-start | bytes 2457600 | tf_op jit(solution)/shard_map/reduce_scatter | solution.py:194
  424.2 57.0 %copy-start.25 = (bf16[192,768]{0,1:T(8,128)(2,1)S(1)}, bf16[192,768]{0,1:T(8,128)(2,1)}, u32[]{:S(2)}) copy-start(bf16[192,768]{0,1:T(8,128)(2,1)} %all_gather.41) | copy-start | bytes 884740
  424.2 57.0 %all-gather.17.cloned.1.call-start = ((), (), s32[]{:S(2)}) async-start(), calls=%async_computation.16 | async-start | bytes 2457600 | tf_op jit(solution)/shard_map/all_gather | solution.py:204
  459.4 225.5 %reduce-scatter.11.cloned.1.call-start = ((), (), s32[]{:S(2)}) async-start(), calls=%async_computation.17 | async-start | bytes 2457600 | tf_op jit(solution)/shard_map/reduce_scatter | solution.py:278
  602.8 30.9 %collective-permute-start.2 = (bf16[1280,384]{0,1:T(8,128)(2,1)S(1)}, bf16[1280,384]{0,1:T(8,128)(2,1)S(1)}, u32[]{:S(2)}, u32[]{:S(2)}) collective-permute-start(bf16[1280,384]{0,1:T(8,128)(2,1)S(1)} %slice.58), channel_id=1, source_target_pairs={{4,0},{8,4},{12,8},{16,12},{20,16},{24,20},{28,24},{5,1},{9,5},{13... | collective-permute-start | bytes 2949128 | tf_op jit(solution)/shard_map/ppermute | solution.py:16
  604.3 29.4 %collective-permute-start.3 = (bf16[256,384]{0,1:T(8,128)(2,1)S(1)}, bf16[256,384]{0,1:T(8,128)(2,1)S(1)}, u32[]{:S(2)}, u32[]{:S(2)}) collective-permute-start(bf16[256,384]{0,1:T(8,128)(2,1)S(1)} %slice.59), channel_id=1, source_target_pairs={{8,0},{12,4},{16,8},{20,12},{24,16},{28,20},{9,1},{13,5},{17,9},{2... | collective-permute-start | bytes 589832 | tf_op jit(solution)/shard_map/ppermute | solution.py:16
  645.7 32.7 %all-to-all-start.3 = ((bf16[8,768,96]{1,2,0:T(8,128)(2,1)}), bf16[8,768,96]{1,2,0:T(8,128)(2,1)}, u32[]{:S(2)}, u32[]{:S(2)}) async-start(bf16[8,768,96]{1,2,0:T(8,128)(2,1)} %bitcast.154), calls=%async_computation.7 | async-start | bytes 2359296 | tf_op jit(solution)/shard_map/all_to_all | solution.py:27
  650.0 84.5 %reduce-scatter.7.cloned.1.call-start = ((), (), s32[]{:S(2)}) async-start(), calls=%async_computation.13 | async-start | bytes 2457600 | tf_op jit(solution)/shard_map/reduce_scatter | solution.py:177
  678.4 17.6 %all-to-all-start.1 = ((bf16[8,192,96]{2,1,0:T(8,128)(2,1)}), bf16[8,192,96]{2,1,0:T(8,128)(2,1)}, u32[]{:S(2)}, u32[]{:S(2)}) async-start(bf16[8,192,96]{2,1,0:T(8,128)(2,1)} %bitcast.150), calls=%async_computation.5 | async-start | bytes 786432 | tf_op jit(solution)/shard_map/all_to_all | solution.py:27
  696.0 30.0 %all-to-all-start = ((bf16[8,96,577]{2,1,0:T(8,128)(2,1)}), bf16[8,96,577]{2,1,0:T(8,128)(2,1)S(1)}, u32[]{:S(2)}, u32[]{:S(2)}) async-start(bf16[8,96,577]{2,1,0:T(8,128)(2,1)} %pad_maximum_fusion.2), calls=%async_computation.4 | async-start | bytes 1966080 | tf_op jit(solution)/shard_map/all_to_all | solution.py:27
  727.0 36.4 %all-to-all-start.2 = ((bf16[8,96,769]{2,1,0:T(8,128)(2,1)}), bf16[8,96,769]{2,1,0:T(8,128)(2,1)S(1)}, u32[]{:S(2)}, u32[]{:S(2)}) async-start(bf16[8,96,769]{2,1,0:T(8,128)(2,1)} %pad_maximum_fusion), calls=%async_computation.6 | async-start | bytes 2752512 | tf_op jit(solution)/shard_map/all_to_all | solution.py:27
  (44 other events, 673.4 us)
Sparse Core Ops, SparseCore 0:
  39.3 19.0 all-gather.6
  270.2 33.4 reduce-scatter.4
  424.4 30.6 reduce-scatter.8
  639.0 28.7 reduce-scatter.10
  670.4 30.8 reduce-scatter.6
Sparse Core Ops, SparseCore 1:
  273.0 44.3 all-gather.10
  319.5 20.1 all-gather.8
  342.0 41.5 all-gather.12
  385.2 20.1 all-gather.14
  459.5 21.7 all-gather.16
where the time goes:
time: 778 us; the launch traced here: 773 us
  waiting for transfers between devices  259 us (33%)
  blocking collectives  170 us (22%)
  matrix products  150 us (19%)
  other arithmetic  107 us (14%)
  local copies, waits for them, and re-layouts  43.4 us (6%)
  starting transfers between devices  24.5 us (3%)
  between operations  17 us (2%)
    all_to_all x4, waiting for transfers between devices, sum_at_owner(): lax.all_to_all(tiles, axis, split_axis=0, concat_axis=0, tiled=True)  51.2 us
    dot_general x4, matrix products, scores_of(): jnp.einsum('qhd,khd->hqk', query_block, key_block, preferred_element_type...  46.3 us
    all_gather x1, blocking collectives, shards(): lax.all_gather(w_out, 'dp', axis=1, tiled=True)  46 us
    all_gather x1, waiting for transfers between devices, shards(): lax.all_gather(w_down, 'dp', axis=1, tiled=True)  38.4 us
    reduce_scatter x1, waiting for transfers between devices, shards(): lax.psum_scatter(jnp.dot(context, full_out, preferred_element_type=jnp.fl...  32.7 us
    all_gather x1, blocking collectives, shards(): lax.all_gather(w_key, 'dp', axis=0, tiled=True)  31.2 us
    all_gather x1, blocking collectives, shards(): lax.all_gather(w_value, 'dp', axis=0, tiled=True)  31.2 us
    all_gather x1, blocking collectives, shards(): lax.all_gather(w_query, 'dp', axis=0, tiled=True)  31 us
  transfers between devices with their start and end apart: 18, of which 12 were waited for; matrix products, arithmetic and copies ran while one was open for 8% of the time, Pallas kernels for 0%

commit v1 on v0

--- a/solution.py
+++ b/solution.py
@@ -72,6 +72,32 @@
     w_up,
     w_down,
 ):
+
+    def answer_heaps(incoming_x):
+        mesh_name = "tensor"
+        mixed_arr = lax.axis_size(mesh_name)
+        low = lax.axis_index(mesh_name)
+        work_now, v_next, u1 = (mixed_arr, low, incoming_x.shape[0])
+        kept_rows = [h * work_now if rr == 0 else h for rr, h in enumerate(incoming_x.shape)]
+        taken_in = jnp.zeros(kept_rows, incoming_x.dtype)
+        item_now = lax.dynamic_update_slice_in_dim(taken_in, incoming_x, v_next * u1, axis=0)
+        arr_next = after = incoming_x
+        for k0 in range(1, work_now // 2 + 1):
+            later = list(map(lambda rr: (rr, (rr + 1) % work_now), range(work_now)))
+            arr_next = lax.ppermute(arr_next, axis_name=mesh_name, perm=later)
+            item_now = lax.dynamic_update_slice_in_dim(
+                item_now, arr_next, (v_next - k0) % work_now * u1, axis=0
+            )
+            if 2 * k0 < work_now:
+                passed = range(work_now)
+                even = map(lambda rr: (rr, (rr - 1) % work_now), passed)
+                known = list(even)
+                after = lax.ppermute(after, axis_name=mesh_name, perm=known)
+                item_now = lax.dynamic_update_slice_in_dim(
+                    item_now, after, (v_next + k0) % work_now * u1, axis=0
+                )
+        return item_now
+
     gain_one, full_query, full_key, full_value, full_out, gain_two, full_up, full_down = (
         lax.all_gather(norm1_gain, "dp", axis=0, tiled=True),
         lax.all_gather(w_query, "dp", axis=0, tiled=True),
@@ -171,7 +197,7 @@
     factor_two = row_scale(middle)
     hat_two = middle * factor_two
     normed_two = (hat_two * gain_two).astype(jnp.bfloat16)
-    normed_two_all = lax.all_gather(normed_two, "tensor", axis=0, tiled=True)
+    normed_two_all = answer_heaps(normed_two)
     upper = jnp.dot(normed_two_all, full_up, preferred_element_type=jnp.float32)
     active = gelu_exact(upper).astype(jnp.bfloat16)
     result = middle + lax.psum_scatter(

time: 778 us -> 753 us (0.968)
  waiting for transfers between devices: 259 us -> 230 us
    all_gather x1 -> x0, waiting for transfers between devices: 22.3 us -> none  [shards(): normed_two_all = lax.all_gather(normed_two, 'tensor', axis=0, tiled=True)]
    ppermute x0 -> x3, waiting for transfers between devices: none -> 17.8 us  [the longest x2 17.8 us: answer_heaps(): arr_next = lax.ppermute(arr_next, axis_name=mesh_name, perm=later)]
    all_gather x1, waiting for transfers between devices: 38.4 us -> 24 us  [shards(): lax.all_gather(w_down, 'dp', axis=1, tiled=True)]
    all_gather x1, waiting for transfers between devices: 8.94 us -> 0.01 us  [shards(): lax.all_gather(w_up, 'dp', axis=0, tiled=True)]
  transfers between devices with their start and end apart: 18 -> 20, of which waited for: 12 -> 12; matrix products, arithmetic and copies ran while one was open for 8% -> 8% of each run, Pallas kernels for 0% -> 0%
where the time goes in v1:
time: 753 us; the launch traced here: 748 us
  waiting for transfers between devices  230 us (31%)
  blocking collectives  170 us (23%)
  matrix products  150 us (20%)
  other arithmetic  107 us (14%)
  local copies, waits for them, and re-layouts  47.3 us (6%)
  starting transfers between devices  26.2 us (3%)
  between operations  16.8 us (2%)
    all_to_all x4, waiting for transfers between devices, sum_at_owner(): lax.all_to_all(tiles, axis, split_axis=0, concat_axis=0, tiled=True)  51.1 us
    dot_general x4, matrix products, scores_of(): jnp.einsum('qhd,khd->hqk', query_block, key_block, preferred_element_type...  46.2 us
    all_gather x1, blocking collectives, shards(): lax.all_gather(w_out, 'dp', axis=1, tiled=True)  46 us
    reduce_scatter x1, waiting for transfers between devices, shards(): lax.psum_scatter(jnp.dot(context, full_out, preferred_element_type=jnp.fl...  31.6 us
    all_gather x1, blocking collectives, shards(): lax.all_gather(w_key, 'dp', axis=0, tiled=True)  31.2 us
    all_gather x1, blocking collectives, shards(): lax.all_gather(w_value, 'dp', axis=0, tiled=True)  31.2 us
    all_gather x1, blocking collectives, shards(): lax.all_gather(w_query, 'dp', axis=0, tiled=True)  31 us
    reduce_scatter x1, waiting for transfers between devices, shards(): lax.psum_scatter(jnp.einsum('tf,cf->tc', grad_upper, full_up, preferred_e...  30.7 us
  transfers between devices with their start and end apart: 20, of which 12 were waited for; matrix products, arithmetic and copies ran while one was open for 8% of the time, Pallas kernels for 0%

profile of v1, /device:TPU:0, one launch (start us, length us, event | category | flops | bytes accessed | tf_op | source)
XLA Modules:
  0.0 747.6 jit_solution(17046863699323357800)
XLA Ops:
  12.9 23.7 %all-reduce.5 = (bf16[768]{0:T(1024)(128)(2,1)S(1)}, bf16[768]{0:T(1024)(128)(2,1)}) all-reduce(bf16[768]{0:T(1024)(128)(2,1)S(1)} %dynamic-update-slice, bf16[768]{0:T(1024)(128)(2,1)S(1)} %dynamic-update-slice.1), channel_id=1, replica_groups=mesh['dp'=8,'tensor'=4] {'dp'}, use_global_device_ids=true, to_apply=%add.2 | all-reduce | flops 1536 | bytes 6144
  41.0 31.2 %all_gather.35 = bf16[768,192]{1,0:T(8,128)(2,1)S(1)} all-gather(bf16[96,192]{1,0:T(8,128)(2,1)} %param.22), channel_id=1, replica_groups=mesh['dp'=8,'tensor'=4] {'dp'}, dimensions={0}, use_global_device_ids=true | all-gather | bytes 331776 | tf_op jit(solution)/shard_map/all_gather | solution.py:104
  72.2 31.2 %all_gather.36 = bf16[768,192]{1,0:T(8,128)(2,1)S(1)} all-gather(bf16[96,192]{1,0:T(8,128)(2,1)} %param.23), channel_id=1, replica_groups=mesh['dp'=8,'tensor'=4] {'dp'}, dimensions={0}, use_global_device_ids=true | all-gather | bytes 331776 | tf_op jit(solution)/shard_map/all_gather | solution.py:105
  110.2 46.0 %all_gather.38 = bf16[192,768]{0,1:T(8,128)(2,1)} all-gather(bf16[192,96]{0,1:T(8,128)(2,1)S(1)} %copy.48), channel_id=1, replica_groups=mesh['dp'=8,'tensor'=4] {'dp'}, dimensions={1}, use_global_device_ids=true | all-gather | bytes 331776 | tf_op jit(solution)/shard_map/all_gather | solution.py:106
  156.2 31.0 %all_gather.37 = bf16[768,192]{1,0:T(8,128)(2,1)S(1)} all-gather(bf16[96,192]{1,0:T(8,128)(2,1)S(1)} %copy-done.36), channel_id=1, replica_groups=mesh['dp'=8,'tensor'=4] {'dp'}, dimensions={0}, use_global_device_ids=true | all-gather | bytes 331776 | tf_op jit(solution)/shard_map/all_gather | solution.py:103
  193.2 72.4 %while.29 = (s32[]{:T(128)}, bf16[2,640,192]{1,2,0:T(8,128)(2,1)}, f32[2,3,640]{2,1,0:T(4,128)S(1)}, s32[2]{0:T(128)S(1)}, bf16[2816,384]{0,1:T(8,128)(2,1)}, /*...) while((s32[]{:T(128)}, bf16[2,640,192]{1,2,0:T(8,128)(2,1)}, ...), condition=%wide.region_6.7_spmd.clone, body=%wide.region_3.6_spmd.clone.sunk | while | flops 1133730560 | bytes 66249560 | solution.py:189
  209.3 10.5 %fusion.137 = f32[3,640]{1,0:T(4,128)S(1)} fusion(f32[3,640,2176]{2,1,0:T(8,128)} %get-tuple-element.568, f32[3,640]{1,0:T(4,128)S(1)} %get-tuple-element.569, pred[640,2176]{1,0:T(8,128)(4,1)S(1)} %fusion.135), kind=kLoop, calls=%fused_computation.8.clone.1 | loop fusion | flops 16709760 | bytes 18119680 | tf_op jit(solution)/shard_map/while/body/eval_jaxpr/reduce_sum | solution.py:181
  245.4 10.5 %fusion.137 = f32[3,640]{1,0:T(4,128)S(1)} fusion(f32[3,640,2176]{2,1,0:T(8,128)} %get-tuple-element.568, f32[3,640]{1,0:T(4,128)S(1)} %get-tuple-element.569, pred[640,2176]{1,0:T(8,128)(4,1)S(1)} %fusion.135), kind=kLoop, calls=%fused_computation.8.clone.1 | loop fusion | flops 16709760 | bytes 18119680 | tf_op jit(solution)/shard_map/while/body/eval_jaxpr/reduce_sum | solution.py:181
  272.1 31.6 %reduce-scatter.5.cloned.1.call-done = bf16[320,768]{1,0:T(8,128)(2,1)} async-done(((bf16[1280,768]{1,0:T(8,128)(2,1)}), bf16[320,768]{1,0:T(8,128)(2,1)}) %reduce-scatter.5.cloned.1.call-update) | async-done | bytes 491536 | tf_op jit(solution)/shard_map/reduce_scatter | solution.py:191
  309.3 11.2 %collective-permute-done.2 = bf16[320,768]{1,0:T(8,128)(2,1)S(1)} collective-permute-done((bf16[320,768]{1,0:T(8,128)(2,1)S(1)}, bf16[320,768]{1,0:T(8,128)(2,1)S(1)}, u32[]{:S(2)}, u32[]{:S(2)}) %collective-permute-start.2) | collective-permute-done | bytes 491552 | tf_op jit(solution)/shard_map/ppermute | solution.py:87
  335.1 24.0 %all-gather.10.cloned.1.call-done = bf16[768,768]{0,1:T(8,128)(2,1)} async-done(((bf16[768,96]{0,1:T(8,128)(2,1)}), bf16[768,768]{0,1:T(8,128)(2,1)}) %all-gather.10.cloned.1.call-update) | async-done | bytes 1179664 | tf_op jit(solution)/shard_map/all_gather | solution.py:109
  359.1 21.6 %all-gather.12.cloned.1.call-done = bf16[1280,768]{1,0:T(8,128)(2,1)} async-done(((bf16[320,768]{1,0:T(8,128)(2,1)}), bf16[1280,768]{1,0:T(8,128)(2,1)}) %all-gather.12.cloned.1.call-update) | async-done | bytes 1966096 | tf_op jit(solution)/shard_map/all_gather | solution.py:210
  380.8 13.1 %add_convert_fusion = (bf16[1280,768]{1,0:T(8,128)(2,1)S(1)}, f32[1280,768]{1,0:T(8,128)}) fusion(f32[1280,768]{1,0:T(8,128)} %fusion.64, bf16[1280,768]{1,0:T(8,128)(2,1)} %all-gather.12.cloned.1.call-done, bf16[768,768]{0,1:T(8,128)(2,1)} %all-gather.10.cloned.1.call-done), kind=kOutput, calls=%fused_computation.47 | convolution fusion | flops 1580728320 | bytes 12976128 | tf_op jit(solution)/shard_map/td,fd->tf/dot_general | solution.py:212
  399.7 30.7 %reduce-scatter.9.cloned.1.call-done = bf16[320,768]{1,0:T(8,128)(2,1)} async-done(((bf16[1280,768]{1,0:T(8,128)(2,1)}), bf16[320,768]{1,0:T(8,128)(2,1)}) %reduce-scatter.9.cloned.1.call-update) | async-done | bytes 491536 | tf_op jit(solution)/shard_map/reduce_scatter | solution.py:220
  435.2 21.4 %all-gather.14.cloned.1.call-done = bf16[1280,768]{1,0:T(8,128)(2,1)} async-done(((bf16[320,768]{1,0:T(8,128)(2,1)}), bf16[1280,768]{1,0:T(8,128)(2,1)}) %all-gather.14.cloned.1.call-update) | async-done | bytes 1966096 | tf_op jit(solution)/shard_map/all_gather | solution.py:230
  462.9 112.5 %while.30 = (s32[]{:T(128)}, bf16[1280,192]{0,1:T(8,128)(2,1)}, f32[2816,384]{0,1:T(8,128)}, bf16[2816,384]{0,1:T(8,128)(2,1)}, s32[2816]{0:T(1024)S(1)}, /*inde...) while((s32[]{:T(128)}, bf16[1280,192]{0,1:T(8,128)(2,1)}, ...), condition=%wide.region_14.15_spmd.clone, body=%wide.region_12.14_spmd.clone.sunk | while | flops 2727729920 | bytes 220916592 | solution.py:279
  478.7 15.1 %multiply_reduce_fusion.3 = (f32[3,640]{1,0:T(4,128)S(1)}, f32[3,640,2176]{2,1,0:T(8,128)}) fusion(f32[3,640,2176]{2,1,0:T(8,128)} %fusion.150, f32[3,640]{1,0:T(4,128)S(1)} %dynamic-slice_bitcast_fusion.2, bf16[640,3,64]{0,2,1:T(8,128)(2,1)S(1)} %bitcast.138, bf16[2176,3,64]{0,2,1:T(8,128)(2,1)S(1)} %bitcast.135, pred[640,2176]{1,0:T(8,128)(4,1)S(1)} %fusion.151), kind=kOutput, calls=%fused_computation.24.clone.1 | convolution fusion | flops 555661440 | bytes 35912704 | tf_op jit(solution)/shard_map/while/body/eval_jaxpr/qhd,khd->hqk/dot_general | solution.py:172
  493.8 11.4 %multiply_convert_fusion.5 = bf16[3,640,2176]{2,1,0:T(8,128)(2,1)S(1)} fusion(f32[3,640,2176]{2,1,0:T(8,128)} %get-tuple-element.585, f32[3,640,2176]{2,1,0:T(8,128)} %fusion.150, f32[3,640]{1,0:T(4,128)S(1)} %get-tuple-element.586), kind=kLoop, calls=%fused_computation.23.clone.1 | loop fusion | flops 12533760 | bytes 41786880 | tf_op jit(solution)/shard_map/while/body/eval_jaxpr/convert_element_type | solution.py:249
  534.9 15.1 %multiply_reduce_fusion.3 = (f32[3,640]{1,0:T(4,128)S(1)}, f32[3,640,2176]{2,1,0:T(8,128)}) fusion(f32[3,640,2176]{2,1,0:T(8,128)} %fusion.150, f32[3,640]{1,0:T(4,128)S(1)} %dynamic-slice_bitcast_fusion.2, bf16[640,3,64]{0,2,1:T(8,128)(2,1)S(1)} %bitcast.138, bf16[2176,3,64]{0,2,1:T(8,128)(2,1)S(1)} %bitcast.135, pred[640,2176]{1,0:T(8,128)(4,1)S(1)} %fusion.151), kind=kOutput, calls=%fused_computation.24.clone.1 | convolution fusion | flops 555661440 | bytes 35912704 | tf_op jit(solution)/shard_map/while/body/eval_jaxpr/qhd,khd->hqk/dot_general | solution.py:172
  550.1 11.4 %multiply_convert_fusion.5 = bf16[3,640,2176]{2,1,0:T(8,128)(2,1)S(1)} fusion(f32[3,640,2176]{2,1,0:T(8,128)} %get-tuple-element.585, f32[3,640,2176]{2,1,0:T(8,128)} %fusion.150, f32[3,640]{1,0:T(4,128)S(1)} %get-tuple-element.586), kind=kLoop, calls=%fused_computation.23.clone.1 | loop fusion | flops 12533760 | bytes 41786880 | tf_op jit(solution)/shard_map/while/body/eval_jaxpr/convert_element_type | solution.py:249
  581.6 27.3 %collective-permute-done.6 = bf16[256,384]{0,1:T(8,128)(2,1)S(1)} collective-permute-done((bf16[256,384]{0,1:T(8,128)(2,1)S(1)}, bf16[256,384]{0,1:T(8,128)(2,1)S(1)}, u32[]{:S(2)}, u32[]{:S(2)}) %collective-permute-start.6) | collective-permute-done | bytes 196640 | tf_op jit(solution)/shard_map/ppermute | solution.py:16
  642.3 11.3 %all-to-all-done.3 = bf16[8,768,96]{1,2,0:T(8,128)(2,1)} async-done(((bf16[8,768,96]{1,2,0:T(8,128)(2,1)}), bf16[8,768,96]{1,2,0:T(8,128)(2,1)}, u32[]{:S(2)}, u32[]{:S(2)}) %all-to-all-start.3) | async-done | bytes 1179680 | tf_op jit(solution)/shard_map/all_to_all | solution.py:27
  685.8 15.5 %all-to-all-done = bf16[8,96,577]{2,1,0:T(8,128)(2,1)S(1)} async-done(((bf16[8,96,577]{2,1,0:T(8,128)(2,1)}), bf16[8,96,577]{2,1,0:T(8,128)(2,1)S(1)}, u32[]{:S(2)}, u32[]{:S(2)}) %all-to-all-start) | async-done | bytes 886304 | tf_op jit(solution)/shard_map/all_to_all | solution.py:27
  714.3 24.3 %all-to-all-done.2 = bf16[8,96,769]{2,1,0:T(8,128)(2,1)S(1)} async-done(((bf16[8,96,769]{2,1,0:T(8,128)(2,1)}), bf16[8,96,769]{2,1,0:T(8,128)(2,1)S(1)}, u32[]{:S(2)}, u32[]{:S(2)}) %all-to-all-start.2) | async-done | bytes 1181216 | tf_op jit(solution)/shard_map/all_to_all | solution.py:27
  (275 shorter events, 259.9 us)
Async XLA Ops:
  8.0 95.4 %all-gather.6.cloned.1.call-start = ((), (), s32[]{:S(2)}) async-start(), calls=%async_computation.8 | async-start | bytes 2457600 | tf_op jit(solution)/shard_map/all_gather | solution.py:127
  39.2 264.4 %reduce-scatter.5.cloned.1.call-start = ((), (), s32[]{:S(2)}) async-start(), calls=%async_computation.9 | async-start | bytes 2457600 | tf_op jit(solution)/shard_map/reduce_scatter | solution.py:191
  105.9 82.6 %copy-start.3 = (bf16[1280,768]{1,0:T(8,128)(2,1)S(1)}, bf16[1280,768]{1,0:T(8,128)(2,1)}, u32[]{:S(2)}) copy-start(bf16[1280,768]{1,0:T(8,128)(2,1)} %all-gather.6.cloned.1.call-done) | copy-start | bytes 5898244
  108.5 83.2 %collective-permute-start.1 = (bf16[1280,384]{0,1:T(8,128)(2,1)S(1)}, bf16[1280,384]{0,1:T(8,128)(2,1)S(1)}, u32[]{:S(2)}, u32[]{:S(2)}) collective-permute-start(bf16[1280,384]{0,1:T(8,128)(2,1)S(1)} %pad_maximum_fusion.1), channel_id=1, source_target_pairs={{0,4},{4,8},{8,12},{12,16},{16,20},{20,24},{24,28},{1,5},{5,9},{9,... | collective-permute-start | bytes 2949128 | tf_op jit(solution)/shard_map/ppermute | solution.py:16
  187.2 4.5 collective-permute-start
  270.0 59.6 %all-gather.8.cloned.1.call-start = ((), (), s32[]{:S(2)}) async-start(), calls=%async_computation.10 | async-start | bytes 1327104 | tf_op jit(solution)/shard_map/all_gather | solution.py:108
  270.6 88.5 %all-gather.10.cloned.1.call-start = ((), (), s32[]{:S(2)}) async-start(), calls=%async_computation.11 | async-start | bytes 1327104 | tf_op jit(solution)/shard_map/all_gather | solution.py:109
  271.2 109.6 %all-gather.12.cloned.1.call-start = ((), (), s32[]{:S(2)}) async-start(), calls=%async_computation.13 | async-start | bytes 2457600 | tf_op jit(solution)/shard_map/all_gather | solution.py:210
  271.8 158.6 %reduce-scatter.9.cloned.1.call-start = ((), (), s32[]{:S(2)}) async-start(), calls=%async_computation.14 | async-start | bytes 2457600 | tf_op jit(solution)/shard_map/reduce_scatter | solution.py:220
  272.0 160.5 %copy-start.30 = (f32[768]{0:T(1024)}, f32[768]{0:T(1024)S(1)}, u32[]{:S(2)}) copy-start(f32[768]{0:T(1024)S(1)} %convert_element_type.159) | copy-start | bytes 9220
  304.9 127.6 %copy-start.34 = (f32[320]{0:T(512)}, f32[320]{0:T(512)S(1)}, u32[]{:S(2)}) copy-start(f32[320]{0:T(512)S(1)} %add_rsqrt_fusion) | copy-start | bytes 3844
  307.6 12.9 %collective-permute-start.2 = (bf16[320,768]{1,0:T(8,128)(2,1)S(1)}, bf16[320,768]{1,0:T(8,128)(2,1)S(1)}, u32[]{:S(2)}, u32[]{:S(2)}) collective-permute-start(bf16[320,768]{1,0:T(8,128)(2,1)S(1)} %get-tuple-element.423), channel_id=1, source_target_pairs={{0,1},{1,2},{2,3},{3,0},{4,5},{5,6},{6,7},{7,4},{8,9},{9,10},{10,1... | collective-permute-start | bytes 1474568 | tf_op jit(solution)/shard_map/ppermute | solution.py:87
  307.6 13.8 %collective-permute-start.3 = (bf16[320,768]{1,0:T(8,128)(2,1)S(1)}, bf16[320,768]{1,0:T(8,128)(2,1)S(1)}, u32[]{:S(2)}, u32[]{:S(2)}) collective-permute-start(bf16[320,768]{1,0:T(8,128)(2,1)S(1)} %get-tuple-element.423), channel_id=1, source_target_pairs={{0,3},{1,0},{2,1},{3,2},{4,7},{5,4},{6,5},{7,6},{8,11},{9,8},{10,9... | collective-permute-start | bytes 1474568 | tf_op jit(solution)/shard_map/ppermute | solution.py:95
  320.5 8.3 %collective-permute-start.4 = (bf16[320,768]{1,0:T(8,128)(2,1)S(1)}, bf16[320,768]{1,0:T(8,128)(2,1)S(1)}, u32[]{:S(2)}, u32[]{:S(2)}) collective-permute-start(bf16[320,768]{1,0:T(8,128)(2,1)S(1)} %collective-permute-done.2), channel_id=1, source_target_pairs={{0,1},{1,2},{2,3},{3,0},{4,5},{5,6},{6,7},{7,4},{8,9},{9,10},{10,1... | collective-permute-start | bytes 1474568 | tf_op jit(solution)/shard_map/ppermute | solution.py:87
  399.6 57.0 %copy-start.25 = (bf16[192,768]{0,1:T(8,128)(2,1)S(1)}, bf16[192,768]{0,1:T(8,128)(2,1)}, u32[]{:S(2)}) copy-start(bf16[192,768]{0,1:T(8,128)(2,1)} %all_gather.38) | copy-start | bytes 884740
  399.6 57.0 %all-gather.14.cloned.1.call-start = ((), (), s32[]{:S(2)}) async-start(), calls=%async_computation.15 | async-start | bytes 2457600 | tf_op jit(solution)/shard_map/all_gather | solution.py:230
  434.8 225.4 %reduce-scatter.11.cloned.1.call-start = ((), (), s32[]{:S(2)}) async-start(), calls=%async_computation.16 | async-start | bytes 2457600 | tf_op jit(solution)/shard_map/reduce_scatter | solution.py:304
  578.0 30.9 %collective-permute-start.5 = (bf16[1280,384]{0,1:T(8,128)(2,1)S(1)}, bf16[1280,384]{0,1:T(8,128)(2,1)S(1)}, u32[]{:S(2)}, u32[]{:S(2)}) collective-permute-start(bf16[1280,384]{0,1:T(8,128)(2,1)S(1)} %slice.58), channel_id=1, source_target_pairs={{4,0},{8,4},{12,8},{16,12},{20,16},{24,20},{28,24},{5,1},{9,5},{13... | collective-permute-start | bytes 2949128 | tf_op jit(solution)/shard_map/ppermute | solution.py:16
  579.5 29.4 %collective-permute-start.6 = (bf16[256,384]{0,1:T(8,128)(2,1)S(1)}, bf16[256,384]{0,1:T(8,128)(2,1)S(1)}, u32[]{:S(2)}, u32[]{:S(2)}) collective-permute-start(bf16[256,384]{0,1:T(8,128)(2,1)S(1)} %slice.59), channel_id=1, source_target_pairs={{8,0},{12,4},{16,8},{20,12},{24,16},{28,20},{9,1},{13,5},{17,9},{2... | collective-permute-start | bytes 589832 | tf_op jit(solution)/shard_map/ppermute | solution.py:16
  620.9 32.7 %all-to-all-start.3 = ((bf16[8,768,96]{1,2,0:T(8,128)(2,1)}), bf16[8,768,96]{1,2,0:T(8,128)(2,1)}, u32[]{:S(2)}, u32[]{:S(2)}) async-start(bf16[8,768,96]{1,2,0:T(8,128)(2,1)} %bitcast.154), calls=%async_computation.7 | async-start | bytes 2359296 | tf_op jit(solution)/shard_map/all_to_all | solution.py:27
  625.2 84.5 %reduce-scatter.7.cloned.1.call-start = ((), (), s32[]{:S(2)}) async-start(), calls=%async_computation.12 | async-start | bytes 2457600 | tf_op jit(solution)/shard_map/reduce_scatter | solution.py:203
  653.6 17.6 %all-to-all-start.1 = ((bf16[8,192,96]{2,1,0:T(8,128)(2,1)}), bf16[8,192,96]{2,1,0:T(8,128)(2,1)}, u32[]{:S(2)}, u32[]{:S(2)}) async-start(bf16[8,192,96]{2,1,0:T(8,128)(2,1)} %bitcast.150), calls=%async_computation.5 | async-start | bytes 786432 | tf_op jit(solution)/shard_map/all_to_all | solution.py:27
  671.3 30.0 %all-to-all-start = ((bf16[8,96,577]{2,1,0:T(8,128)(2,1)}), bf16[8,96,577]{2,1,0:T(8,128)(2,1)S(1)}, u32[]{:S(2)}, u32[]{:S(2)}) async-start(bf16[8,96,577]{2,1,0:T(8,128)(2,1)} %pad_maximum_fusion.2), calls=%async_computation.4 | async-start | bytes 1966080 | tf_op jit(solution)/shard_map/all_to_all | solution.py:27
  702.2 36.4 %all-to-all-start.2 = ((bf16[8,96,769]{2,1,0:T(8,128)(2,1)}), bf16[8,96,769]{2,1,0:T(8,128)(2,1)S(1)}, u32[]{:S(2)}, u32[]{:S(2)}) async-start(bf16[8,96,769]{2,1,0:T(8,128)(2,1)} %pad_maximum_fusion), calls=%async_computation.6 | async-start | bytes 2752512 | tf_op jit(solution)/shard_map/all_to_all | solution.py:27
  (47 other events, 779.4 us)
Sparse Core Ops, SparseCore 0:
  39.3 19.0 all-gather.5
  270.1 33.4 reduce-scatter.4
  399.7 30.6 reduce-scatter.8
Sparse Core Ops, SparseCore 1:
  272.7 44.3 all-gather.7
  319.1 40.0 all-gather.9
  360.6 20.1 all-gather.11
  434.9 21.7 all-gather.13
  614.2 28.7 reduce-scatter.10
  645.7 30.8 reduce-scatter.6
